TPU v7x, 32 devices: a whole 2x2x4 slice. The times are simulated.
32 devices in a mesh: panel: 4 (over z), tx: 2 (over y), ty: 4 (over x, core).
Axes of the slice: x: 2, y: 2, z: 4, core: 2. Of those that a mesh axis runs over, the one named last changes fastest.
Arguments:
- cotangent: float32 [70, 64, 512], P(None, ('panel', 'tx'), 'ty'), may hold values from -30 to 30
- courant: float32 [70, 64, 512], P(None, ('panel', 'tx'), 'ty'), may hold values from 0.1 to 0.9
- faces_first: float32 [70, 64, 512], P(None, ('panel', 'tx'), 'ty'), may hold values from 0.1 to 1
- faces_second: float32 [70, 64, 512], P(None, ('panel', 'tx'), 'ty'), may hold values from 0.1 to 1
- faces_vertical: float32 [69, 64, 512], P(None, ('panel', 'tx'), 'ty'), may hold values from 0.5 to 8
- damping: float32 [70, 64, 512], P(None, ('panel', 'tx'), 'ty'), may hold values from 0.0005 to 0.005
- blocks_fine: float32 [7, 10, 10, 64, 512], P(None, None, None, ('panel', 'tx'), 'ty'), may hold values from 0 to 4
- blocks_half: float32 [7, 10, 10, 32, 256], P(None, None, None, ('panel', 'tx'), 'ty'), may hold values from 0 to 4
- blocks_quarter: float32 [7, 10, 10, 16, 128], P(None, None, None, ('panel', 'tx'), 'ty'), may hold values from 0 to 4
- blocks_eighth: float32 [7, 10, 10, 8, 64], P(None, None, None, ('panel', 'tx'), 'ty'), may hold values from 0 to 4
Outputs:
- solution: float32 [70, 64, 512], P(None, ('panel', 'tx'), 'ty')
- residual: float32 [70, 64, 512], P(None, ('panel', 'tx'), 'ty')
All inputs are finite; a program needn't handle non-finite values.
Results may differ from a plain program's by a relative error of at most 0.0003.
Values sent between devices are 32-bit elements; how exact they have to be, the bound alone decides.
A program may use at most 128 MiB of HBM per device.

v0:
```python
import functools

import jax
import jax.numpy as jnp
from jax import lax
from jax.experimental import pallas as pl
from jax.experimental.pallas import tpu as pltpu
from jax.sharding import PartitionSpec as P

GRIDS = 4
ITERS = 3
OMEGA = 0.8
KEEP = 1.0 - OMEGA
MESH = pl.DeviceIdType.MESH
F32 = jnp.float32


def kernel(
    sizes, count, width,
    cot, cour, ff, fs, fv, damp,
    sol, res,
    M, E, UF, LF, US, LS, C, D, DD, R, X, Z, IM, AL, DR,
    SR, SC, RR, RC, XR, XC, WR, WC, AS, AB,
    s_sem, r_sem, as_sem, ar_sem,
):
    npan, ntx, nty = sizes
    rows, cols = cot.shape[1], cot.shape[2]
    tile = (rows, cols)
    levels = count * width
    na = npan * ntx
    devices = na * nty
    a_me = lax.axis_index("panel") * ntx + lax.axis_index("tx")
    b_me = lax.axis_index("ty")
    me = a_me * nty + b_me

    def place(a, b):
        return (a // ntx, a % ntx, b)

    up_dev = place((a_me + 1) % na, b_me)
    dn_dev = place((a_me + na - 1) % na, b_me)
    rt_dev = place(a_me, (b_me + 1) % nty)
    lf_dev = place(a_me, (b_me + nty - 1) % nty)

    def other(d):
        t = (me + d) % devices
        return place(t // nty, t % nty)

    barrier = pltpu.get_barrier_semaphore()

    @pl.loop(1, devices)
    def _(d):
        pl.semaphore_signal(barrier, inc=1, device_id=other(d), device_id_type=MESH)

    row = lax.broadcasted_iota(jnp.int32, tile, 0)
    lane = lax.broadcasted_iota(jnp.int32, tile, 1)
    zero = jnp.zeros(tile, F32)
    has_left = (b_me > 0).astype(F32)
    has_right = (b_me < nty - 1).astype(F32)

    def bc_row(v):
        return jnp.broadcast_to(v, tile)

    def roll(v, by, axis):
        by = by % tile[axis]
        return v if by == 0 else pltpu.roll(v, by, axis)

    def next_first(v, h, s):
        return jnp.where(row >= rows - s, bc_row(h), roll(v, -s, 0))

    def prev_first(v, h, s):
        return jnp.where(row < s, bc_row(h), roll(v, s, 0))

    def next_second(v, h, s):
        return jnp.where(lane >= cols - s, bc_row(h), roll(v, -s, 1))

    def prev_second(v, h, s):
        return jnp.where(lane < s, bc_row(h), roll(v, s, 1))

    def partner(v, s, axis):
        at = row if axis == 0 else lane
        return jnp.where((at & s) != 0, roll(v, s, axis), roll(v, -s, axis))

    def pair_sum(v, s, axis):
        return v + partner(v, s, axis)

    def pick(v, s, axis, odd):
        at = row if axis == 0 else lane
        keep = ((at & s) != 0) == odd
        return jnp.where(keep, v, partner(v, s, axis))

    def loop(body, carry):
        return lax.fori_loop(0, count, body, carry)

    def pack(slot, l, v, acc):
        lo, hi = acc
        SR[slot, 0, pl.ds(l, 1), :] = v[rows - 1:, :]
        SR[slot, 1, pl.ds(l, 1), :] = v[:1, :]
        lo = jnp.where(lane == l, bc_row(v[:, cols - 1:]), lo)
        hi = jnp.where(lane == l, bc_row(v[:, :1]), hi)
        return lo, hi

    def pack_end(slot, acc):
        SC[slot, 0] = acc[0]
        SC[slot, 1] = acc[1]

    def copies(slot):
        out = []
        for way, dev in ((0, up_dev), (1, dn_dev)):
            out.append(pltpu.make_async_remote_copy(
                SR.at[slot, way], RR.at[slot, way],
                s_sem.at[slot, way], r_sem.at[slot, way], device_id=dev, device_id_type=MESH))
        for way, dev in ((0, rt_dev), (1, lf_dev)):
            out.append(pltpu.make_async_remote_copy(
                SC.at[slot, way], RC.at[slot, way],
                s_sem.at[slot, 2 + way], r_sem.at[slot, 2 + way], device_id=dev, device_id_type=MESH))
        return out

    def start(slot):
        for c in copies(slot):
            c.start()

    def finish(slot):
        for c in copies(slot):
            c.wait()
        RC[slot, 0] = RC[slot, 0] * has_left
        RC[slot, 1] = RC[slot, 1] * has_right

    def exchange(slot):
        start(slot)
        finish(slot)

    def turn(v, k):
        return pltpu.roll(v, (cols - k * width) % cols, 1)

    def coupled(g, k, xs, rows_in, cols_lo, cols_hi, full):
        s = 1 << g
        base = k * width
        clo, chi = turn(cols_lo, k), turn(cols_hi, k)
        out = []
        for a in range(width):
            l = base + a
            v = xs[a]
            h = UF[g, l] * next_first(v, rows_in(1, l), s)
            h = h + LF[g, l] * prev_first(v, rows_in(0, l), s)
            h = h + US[g, l] * next_second(v, chi[:, a:a + 1], s)
            h = h + LS[g, l] * prev_second(v, clo[:, a:a + 1], s)
            out.append(h)
        return out

    def solve(g, k, rs):
        base = k * width
        ys = [rs[0]]
        for a in range(1, width):
            ys.append(rs[a] + M[g, base + a] * ys[-1])
        xs = [None] * width
        xs[-1] = E[g, base + width - 1] * ys[-1]
        for a in range(width - 2, -1, -1):
            xs[a] = E[g, base + a] * ys[a] + M[g, base + a + 1] * xs[a + 1]
        return xs

    def recv_rows(slot):
        return lambda way, l: RR[slot, way, pl.ds(l, 1), :]

    def kept_rows(way, l):
        return XR[way, pl.ds(l, 1), :]

    def across(g, k, field, hs):
        base = k * width
        hs[0] = hs[0] + C[g, base] * field[base]
        hs[-1] = hs[-1] + C[g, base + width] * field[base + width + 1]
        return hs

    def edges(k, acc):
        lo, hi = acc
        for a in range(width):
            l = k * width + a
            SR[0, 0, pl.ds(l, 1), :] = ff[l, rows - 1:, :]
            SR[0, 1, pl.ds(l, 1), :] = ff[l, :1, :]
            w = fs[l]
            lo = jnp.where(lane == l, bc_row(w[:, cols - 1:]), lo)
            hi = jnp.where(lane == l, bc_row(w[:, :1]), hi)
        return lo, hi

    pack_end(0, loop(edges, (zero, zero)))
    for slot in range(2):
        for way in range(2):
            SR[slot, way, pl.ds(levels, SR.shape[2] - levels), :] = jnp.zeros(
                (SR.shape[2] - levels, cols), F32)
    pl.semaphore_wait(barrier, devices - 1)
    start(0)

    for g in range(GRIDS):
        C[g, 0] = zero
        C[g, levels] = zero
        X[g, 0] = zero
        X[g, levels + 1] = zero
    Z[0] = zero
    Z[levels + 1] = zero

    @pl.loop(0, levels - 1)
    def _(l):
        C[0, l + 1] = fv[l]
        res[l] = (1.0 - cour[l]) * cot[l] + cour[l + 1] * cot[l + 1]

    last = levels - 1
    res[last] = (1.0 - cour[last]) * cot[last]

    @pl.loop(0, levels)
    def _(l):
        sol[l] = zero
        AL[l] = zero
        DR[l] = zero

    WR[...] = jnp.zeros(WR.shape, F32)
    WC[...] = jnp.zeros(WC.shape, F32)
    finish(0)

    def grid0(k, carry):
        clo = turn(RC[0, 0], k)
        for a in range(width):
            l = k * width + a
            UF[0, l] = ff[l]
            LF[0, l] = prev_first(ff[l], RR[0, 0, pl.ds(l, 1), :], 1)
            US[0, l] = fs[l]
            LS[0, l] = prev_second(fs[l], clo[:, a:a + 1], 1)
            DD[l] = damp[l]
        return carry

    loop(grid0, 0)

    def factor(g):
        def body(k, carry):
            e = None
            for a in range(width):
                l = k * width + a
                d = DD[l] + UF[g, l] + LF[g, l] + US[g, l] + LS[g, l] + C[g, l] + C[g, l + 1]
                if g == 0:
                    D[l] = d
                if a > 0:
                    m = C[g, l] * e
                    M[g, l] = m
                    d = d - C[g, l] * m
                e = 1.0 / d
                E[g, l] = OMEGA * e
            return carry
        loop(body, 0)

    def coarsen(g):
        s = 1 << g
        def body(k, carry):
            for a in range(width):
                l = k * width + a
                UF[g + 1, l] = pick(pair_sum(UF[g, l], s, 1), s, 0, True)
                LF[g + 1, l] = pick(pair_sum(LF[g, l], s, 1), s, 0, False)
                US[g + 1, l] = pick(pair_sum(US[g, l], s, 0), s, 1, True)
                LS[g + 1, l] = pick(pair_sum(LS[g, l], s, 0), s, 1, False)
                C[g + 1, l + 1] = pair_sum(pair_sum(C[g, l + 1], s, 1), s, 0)
                DD[l] = pair_sum(pair_sum(DD[l], s, 1), s, 0)
            return carry
        loop(body, 0)

    factor(0)
    for g in range(GRIDS - 1):
        coarsen(g)
        factor(g + 1)

    def first(g, slot):
        source = res if g == 0 else R.at[g - 1]
        def body(k, acc):
            base = k * width
            xs = solve(g, k, [source[base + a] for a in range(width)])
            for a in range(width):
                X[g, base + a + 1] = xs[a]
                if slot is not None:
                    acc = pack(slot, base + a, xs[a], acc)
            return acc
        acc = loop(body, (zero, zero) if slot is not None else 0)
        if slot is not None:
            pack_end(slot, acc)

    def remainder(g, rows_in, cols_in):
        s = 1 << g
        source = res if g == 0 else R.at[g - 1]
        clo, chi = cols_in(0), cols_in(1)
        def body(k, carry):
            base = k * width
            xs = [X[g, base + a + 1] for a in range(width)]
            hs = across(g, k, X.at[g], coupled(g, k, xs, rows_in, clo, chi, False))
            for a in range(width):
                v = KEEP * source[base + a] + hs[a]
                R[g, base + a] = pair_sum(pair_sum(v, s, 1), s, 0)
            return carry
        loop(body, 0)

    def last_half(g, slot, out_slot):
        source = res if g == 0 else R.at[g - 1]
        clo, chi = RC[slot, 0], RC[slot, 1]
        rows_in = recv_rows(slot)
        def body(k, acc):
            base = k * width
            xs = [X[g, base + a + 1] for a in range(width)]
            hs = across(g, k, X.at[g], coupled(g, k, xs, rows_in, clo, chi, False))
            zs = solve(g, k, [source[base + a] + hs[a] for a in range(width)])
            for a in range(width):
                z = KEEP * xs[a] + zs[a]
                if g > 0:
                    z = X[g - 1, base + a + 1] + z
                    X[g - 1, base + a + 1] = z
                else:
                    Z[base + a + 1] = z
                acc = pack(out_slot, base + a, z, acc)
            return acc
        pack_end(out_slot, loop(body, (zero, zero)))

    def image(slot, out_slot):
        clo, chi = RC[slot, 0], RC[slot, 1]
        rows_in = recv_rows(slot)
        def body(k, acc):
            rz, iz, pk = acc
            base = k * width
            zs = [Z[base + a + 1] for a in range(width)]
            hs = coupled(0, k, zs, rows_in, clo, chi, True)
            ims = []
            for a in range(width):
                l = base + a
                v = D[l] * zs[a] - hs[a]
                v = v - C[0, l] * Z[l] - C[0, l + 1] * Z[l + 2]
                IM[l] = v
                ims.append(v)
                rz = rz + res[l] * zs[a]
                iz = iz + v * zs[a]
            ws = solve(0, k, ims)
            for a in range(width):
                pk = pack(out_slot, base + a, ws[a], pk)
            return rz, iz, pk
        rz, iz, pk = loop(body, (zero, zero, (zero, zero)))
        pack_end(out_slot, pk)
        return rz, iz

    def sum_copy(it, d):
        return pltpu.make_async_remote_copy(
            AS, AB.at[it, me], as_sem.at[d - 1], ar_sem.at[d - 1],
            device_id=other(d), device_id_type=MESH)

    first(0, 1)
    exchange(1)
    XR[...] = RR[1]
    XC[...] = RC[1]

    def iteration(it, carry):
        gamma, alpha = carry
        remainder(0, kept_rows, lambda way: XC[way])
        for g in range(1, GRIDS):
            slot = (g - 1) % 2
            first(g, slot)
            exchange(slot)
            if g < GRIDS - 1:
                remainder(g, recv_rows(slot), lambda way: RC[slot, way])
        for g in range(GRIDS - 1, -1, -1):
            last_half(g, slot, 1 - slot)
            slot = 1 - slot
            exchange(slot)
        rz, iz = image(slot, 1 - slot)
        slot = 1 - slot
        start(slot)
        top = jnp.sum(rz, axis=0, keepdims=True)
        bot = jnp.sum(iz, axis=0, keepdims=True)
        own = jnp.where(row == 0, bc_row(top), jnp.where(row == 1, bc_row(bot), 0.0))
        AS[...] = own
        AB[it, me] = own

        @pl.loop(1, devices)
        def _(d):
            sum_copy(it, d).start()

        finish(slot)

        @pl.loop(1, devices)
        def _(d):
            sum_copy(it, d).wait()

        total = lax.fori_loop(0, devices, lambda d, t: t + AB[it, d], zero)
        total = jnp.sum(total, axis=1, keepdims=True)
        fresh = bc_row(total[:1])
        curv = bc_row(total[1:2])
        ratio = jnp.where(it == 0, 0.0, fresh / gamma)
        alpha = fresh / (curv - ratio * fresh / alpha)

        @pl.loop(0, count)
        def _(k):
            for a in range(width):
                l = k * width + a
                d = Z[l + 1] + ratio * DR[l]
                DR[l] = d
                sol[l] = sol[l] + alpha * d
                w = IM[l] + ratio * AL[l]
                AL[l] = w
                res[l] = res[l] - alpha * w

        @pl.when(it < ITERS - 1)
        def _():
            for way in range(2):
                w = RC[slot, way] + ratio * WC[way]
                WC[way] = w
                XC[way] = XC[way] - alpha * w
                for t in range(SR.shape[2] // rows):
                    at = pl.ds(t * rows, rows)
                    w = RR[slot, way, at, :] + ratio * WR[way, at, :]
                    WR[way, at, :] = w
                    XR[way, at, :] = XR[way, at, :] - alpha * w
            first(0, None)

        return fresh, alpha

    one = jnp.ones(tile, F32)
    lax.fori_loop(0, ITERS, iteration, (one, one))


def per_device(sizes, cotangent, courant, faces_first, faces_second, faces_vertical, damping, fine, *rest):
    levels, rows, cols = cotangent.shape
    count, width = fine.shape[0], fine.shape[1]
    devices = sizes[0] * sizes[1] * sizes[2]
    padded = -(-levels // rows) * rows
    if levels > cols or rows != 1 << (GRIDS - 1):
        raise ValueError("unsupported tile")
    field = jax.ShapeDtypeStruct((levels, rows, cols), F32)

    def vm(*lead):
        return pltpu.VMEM(lead + (rows, cols), F32)

    vmem = pl.BlockSpec(memory_space=pltpu.VMEM)
    return pl.pallas_call(
        functools.partial(kernel, sizes, count, width),
        out_shape=(field, field),
        in_specs=[vmem] * 6,
        out_specs=(vmem, vmem),
        scratch_shapes=[
            vm(GRIDS, levels), vm(GRIDS, levels),
            vm(GRIDS, levels), vm(GRIDS, levels), vm(GRIDS, levels), vm(GRIDS, levels),
            vm(GRIDS, levels + 1), vm(levels), vm(levels),
            vm(GRIDS - 1, levels), vm(GRIDS, levels + 2), vm(levels + 2),
            vm(levels), vm(levels), vm(levels),
            pltpu.VMEM((2, 2, padded, cols), F32), vm(2, 2),
            pltpu.VMEM((2, 2, padded, cols), F32), vm(2, 2),
            pltpu.VMEM((2, padded, cols), F32), vm(2),
            pltpu.VMEM((2, padded, cols), F32), vm(2),
            vm(), vm(ITERS, devices),
            pltpu.SemaphoreType.DMA((2, 4)), pltpu.SemaphoreType.DMA((2, 4)),
            pltpu.SemaphoreType.DMA((devices - 1,)), pltpu.SemaphoreType.DMA((devices - 1,)),
        ],
        compiler_params=pltpu.CompilerParams(
            collective_id=0, has_side_effects=True, vmem_limit_bytes=48 * 1024 * 1024),
    )(cotangent, courant, faces_first, faces_second, faces_vertical, damping)


def solution(mesh):
    sizes = tuple(mesh.shape[name] for name in ("panel", "tx", "ty"))
    field = P(None, ("panel", "tx"), "ty")
    block = P(None, None, None, ("panel", "tx"), "ty")
    return jax.shard_map(
        functools.partial(per_device, sizes),
        mesh=mesh,
        in_specs=(field,) * 6 + (block,) * 4,
        out_specs=(field, field),
        check_vma=False,
    )
```

profile of v0, /device:TPU:0, one launch (start us, length us, event | category | flops | bytes accessed | tf_op | source)
XLA Modules:
  0.0 194.9 jit_solution(15027566272727409175)
XLA Ops:
  0.6 0.0 copy-start
  0.6 0.9 copy-done
  1.6 0.0 copy-start.1
  1.6 1.0 copy-done.1
  2.5 0.0 copy-start.2
  2.6 1.0 copy-done.2
  3.5 0.0 copy-start.3
  3.5 1.0 copy-done.3
  4.5 0.0 copy-start.4
  4.5 1.0 copy-done.4
  5.4 0.0 copy-start.5
  5.4 1.0 copy-done.5
  6.4 187.1 %shard_map.77 = (f32[70,8,128]{2,1,0:T(8,128)S(1)}, f32[70,8,128]{2,1,0:T(8,128)S(1)}) custom-call(f32[70,8,128]{2,1,0:T(8,128)S(1)} %copy-done, f32[70,8,128]{2,1,0:T(8,128)S(1)} %copy-done.1, f32[70,8,128]{2,1,0:T(8,128)S(1)} %copy-done.2, f32[70,8,128]{2,1,0:T(8,128)S(1)} %copy-done.3, f32[69,8,128]{2,1,0:T(8,128)S(1)} %copy-done.5, ...), custom_call_target="tpu_custom_call" | custom-call | tf_op jit(solution)/shard_map/pallas_call | solution.py:432
  193.5 0.7 copy.10
  194.2 0.7 copy.11
Async XLA Ops:
  0.6 1.0 copy-start
  1.6 1.0 copy-start.1
  2.5 1.0 copy-start.2
  3.5 1.0 copy-start.3
  4.5 1.0 copy-start.4
  5.4 1.0 copy-start.5
where the time goes:
time: 195 us
  Pallas kernels  187 us (96%)
  local copies, waits for them, and re-layouts  7.16 us (4%)
    pallas_call x1, Pallas kernels, per_device(): pl.pallas_call(functools.partial(kernel, sizes, count, width), out_shape=...  187 us
    unnamed x14, local copies, waits for them, and re-layouts  7.16 us

commit v1 on v0

--- a/solution.py
+++ b/solution.py
@@ -20,7 +20,7 @@
     cot, cour, ff, fs, fv, damp,
     sol, res,
     M, E, UF, LF, US, LS, C, D, DD, R, X, Z, IM, AL, DR,
-    SR, SC, RR, RC, XR, XC, WR, WC, AS, AB,
+    SR, SC, RR, RC, QC, XR, XC, WR, WC, AS, AB,
     s_sem, r_sem, as_sem, ar_sem,
 ):
     npan, ntx, nty = sizes
@@ -71,10 +71,10 @@
         return jnp.where(row < s, bc_row(h), roll(v, s, 0))
 
     def next_second(v, h, s):
-        return jnp.where(lane >= cols - s, bc_row(h), roll(v, -s, 1))
+        return jnp.where(lane >= cols - s, h, roll(v, -s, 1))
 
     def prev_second(v, h, s):
-        return jnp.where(lane < s, bc_row(h), roll(v, s, 1))
+        return jnp.where(lane < s, h, roll(v, s, 1))
 
     def partner(v, s, axis):
         at = row if axis == 0 else lane
@@ -89,61 +89,78 @@
         return jnp.where(keep, v, partner(v, s, axis))
 
     def loop(body, carry):
-        return lax.fori_loop(0, count, body, carry)
-
-    def pack(slot, l, v, acc):
-        lo, hi = acc
+        for k in range(count):
+            carry = body(k, carry)
+        return carry
+
+    def tiling(g):
+        per = cols // (2 << g)
+        return per, -(-levels // per)
+
+    def pack_cols(slot, g, l, v, acc):
+        s = 1 << g
+        per, _ = tiling(g)
+        t, m = l // per, l % per
+        moved = roll(v, 2 * s * m + s, 1)
+        if m == 0:
+            acc = jnp.where(lane < 2 * s, moved, 0.0)
+        else:
+            acc = jnp.where((lane >= 2 * s * m) & (lane < 2 * s * (m + 1)), moved, acc)
+        if m == per - 1 or l == levels - 1:
+            SC[slot, t] = acc
+        return acc
+
+    def pack(slot, g, l, v, acc):
         SR[slot, 0, pl.ds(l, 1), :] = v[rows - 1:, :]
         SR[slot, 1, pl.ds(l, 1), :] = v[:1, :]
-        lo = jnp.where(lane == l, bc_row(v[:, cols - 1:]), lo)
-        hi = jnp.where(lane == l, bc_row(v[:, :1]), hi)
-        return lo, hi
-
-    def pack_end(slot, acc):
-        SC[slot, 0] = acc[0]
-        SC[slot, 1] = acc[1]
-
-    def copies(slot):
+        return pack_cols(slot, g, l, v, acc)
+
+    def copies(slot, g):
         out = []
         for way, dev in ((0, up_dev), (1, dn_dev)):
             out.append(pltpu.make_async_remote_copy(
                 SR.at[slot, way], RR.at[slot, way],
                 s_sem.at[slot, way], r_sem.at[slot, way], device_id=dev, device_id_type=MESH))
+        some = pl.ds(0, tiling(g)[1])
         for way, dev in ((0, rt_dev), (1, lf_dev)):
             out.append(pltpu.make_async_remote_copy(
-                SC.at[slot, way], RC.at[slot, way],
+                SC.at[slot, some], RC.at[slot, way, some],
                 s_sem.at[slot, 2 + way], r_sem.at[slot, 2 + way], device_id=dev, device_id_type=MESH))
         return out
 
-    def start(slot):
-        for c in copies(slot):
+    def start(slot, g):
+        for c in copies(slot, g):
             c.start()
 
-    def finish(slot):
-        for c in copies(slot):
+    def finish(slot, g):
+        for c in copies(slot, g):
             c.wait()
-        RC[slot, 0] = RC[slot, 0] * has_left
-        RC[slot, 1] = RC[slot, 1] * has_right
-
-    def exchange(slot):
-        start(slot)
-        finish(slot)
-
-    def turn(v, k):
-        return pltpu.roll(v, (cols - k * width) % cols, 1)
-
-    def coupled(g, k, xs, rows_in, cols_lo, cols_hi, full):
+        s = 1 << g
+        for t in range(tiling(g)[1]):
+            low = RC[slot, 0, t] * has_left
+            high = RC[slot, 1, t] * has_right
+            QC[t] = jnp.where((lane & s) != 0, roll(high, -2 * s, 1), low)
+
+    def exchange(slot, g):
+        start(slot, g)
+        finish(slot, g)
+
+    def beside(source, g, l):
+        per, _ = tiling(g)
+        return roll(source[l // per], -(2 << g) * (l % per), 1)
+
+    def coupled(g, k, xs, rows_in, cols_in):
         s = 1 << g
         base = k * width
-        clo, chi = turn(cols_lo, k), turn(cols_hi, k)
         out = []
         for a in range(width):
             l = base + a
             v = xs[a]
+            q = beside(cols_in, g, l)
             h = UF[g, l] * next_first(v, rows_in(1, l), s)
             h = h + LF[g, l] * prev_first(v, rows_in(0, l), s)
-            h = h + US[g, l] * next_second(v, chi[:, a:a + 1], s)
-            h = h + LS[g, l] * prev_second(v, clo[:, a:a + 1], s)
+            h = h + US[g, l] * next_second(v, q, s)
+            h = h + LS[g, l] * prev_second(v, q, s)
             out.append(h)
         return out
 
@@ -171,23 +188,20 @@
         return hs
 
     def edges(k, acc):
-        lo, hi = acc
         for a in range(width):
             l = k * width + a
             SR[0, 0, pl.ds(l, 1), :] = ff[l, rows - 1:, :]
             SR[0, 1, pl.ds(l, 1), :] = ff[l, :1, :]
-            w = fs[l]
-            lo = jnp.where(lane == l, bc_row(w[:, cols - 1:]), lo)
-            hi = jnp.where(lane == l, bc_row(w[:, :1]), hi)
-        return lo, hi
-
-    pack_end(0, loop(edges, (zero, zero)))
+            acc = pack_cols(0, 0, l, fs[l], acc)
+        return acc
+
+    loop(edges, zero)
     for slot in range(2):
         for way in range(2):
             SR[slot, way, pl.ds(levels, SR.shape[2] - levels), :] = jnp.zeros(
                 (SR.shape[2] - levels, cols), F32)
     pl.semaphore_wait(barrier, devices - 1)
-    start(0)
+    start(0, 0)
 
     for g in range(GRIDS):
         C[g, 0] = zero
@@ -213,16 +227,15 @@
 
     WR[...] = jnp.zeros(WR.shape, F32)
     WC[...] = jnp.zeros(WC.shape, F32)
-    finish(0)
+    finish(0, 0)
 
     def grid0(k, carry):
-        clo = turn(RC[0, 0], k)
         for a in range(width):
             l = k * width + a
             UF[0, l] = ff[l]
             LF[0, l] = prev_first(ff[l], RR[0, 0, pl.ds(l, 1), :], 1)
             US[0, l] = fs[l]
-            LS[0, l] = prev_second(fs[l], clo[:, a:a + 1], 1)
+            LS[0, l] = prev_second(fs[l], beside(QC, 0, l), 1)
             DD[l] = damp[l]
         return carry
 
@@ -272,20 +285,17 @@
             for a in range(width):
                 X[g, base + a + 1] = xs[a]
                 if slot is not None:
-                    acc = pack(slot, base + a, xs[a], acc)
+                    acc = pack(slot, g, base + a, xs[a], acc)
             return acc
-        acc = loop(body, (zero, zero) if slot is not None else 0)
-        if slot is not None:
-            pack_end(slot, acc)
+        loop(body, zero)
 
     def remainder(g, rows_in, cols_in):
         s = 1 << g
         source = res if g == 0 else R.at[g - 1]
-        clo, chi = cols_in(0), cols_in(1)
         def body(k, carry):
             base = k * width
             xs = [X[g, base + a + 1] for a in range(width)]
-            hs = across(g, k, X.at[g], coupled(g, k, xs, rows_in, clo, chi, False))
+            hs = across(g, k, X.at[g], coupled(g, k, xs, rows_in, cols_in))
             for a in range(width):
                 v = KEEP * source[base + a] + hs[a]
                 R[g, base + a] = pair_sum(pair_sum(v, s, 1), s, 0)
@@ -294,12 +304,11 @@
 
     def last_half(g, slot, out_slot):
         source = res if g == 0 else R.at[g - 1]
-        clo, chi = RC[slot, 0], RC[slot, 1]
         rows_in = recv_rows(slot)
         def body(k, acc):
             base = k * width
             xs = [X[g, base + a + 1] for a in range(width)]
-            hs = across(g, k, X.at[g], coupled(g, k, xs, rows_in, clo, chi, False))
+            hs = across(g, k, X.at[g], coupled(g, k, xs, rows_in, QC))
             zs = solve(g, k, [source[base + a] + hs[a] for a in range(width)])
             for a in range(width):
                 z = KEEP * xs[a] + zs[a]
@@ -308,18 +317,17 @@
                     X[g - 1, base + a + 1] = z
                 else:
                     Z[base + a + 1] = z
-                acc = pack(out_slot, base + a, z, acc)
+                acc = pack(out_slot, max(g - 1, 0), base + a, z, acc)
             return acc
-        pack_end(out_slot, loop(body, (zero, zero)))
+        loop(body, zero)
 
     def image(slot, out_slot):
-        clo, chi = RC[slot, 0], RC[slot, 1]
         rows_in = recv_rows(slot)
         def body(k, acc):
             rz, iz, pk = acc
             base = k * width
             zs = [Z[base + a + 1] for a in range(width)]
-            hs = coupled(0, k, zs, rows_in, clo, chi, True)
+            hs = coupled(0, k, zs, rows_in, QC)
             ims = []
             for a in range(width):
                 l = base + a
@@ -331,10 +339,9 @@
                 iz = iz + v * zs[a]
             ws = solve(0, k, ims)
             for a in range(width):
-                pk = pack(out_slot, base + a, ws[a], pk)
+                pk = pack(out_slot, 0, base + a, ws[a], pk)
             return rz, iz, pk
-        rz, iz, pk = loop(body, (zero, zero, (zero, zero)))
-        pack_end(out_slot, pk)
+        rz, iz, pk = loop(body, (zero, zero, zero))
         return rz, iz
 
     def sum_copy(it, d):
@@ -343,26 +350,27 @@
             device_id=other(d), device_id_type=MESH)
 
     first(0, 1)
-    exchange(1)
+    exchange(1, 0)
     XR[...] = RR[1]
-    XC[...] = RC[1]
+    for t in range(tiling(0)[1]):
+        XC[t] = QC[t]
 
     def iteration(it, carry):
         gamma, alpha = carry
-        remainder(0, kept_rows, lambda way: XC[way])
+        remainder(0, kept_rows, XC)
         for g in range(1, GRIDS):
             slot = (g - 1) % 2
             first(g, slot)
-            exchange(slot)
+            exchange(slot, g)
             if g < GRIDS - 1:
-                remainder(g, recv_rows(slot), lambda way: RC[slot, way])
+                remainder(g, recv_rows(slot), QC)
         for g in range(GRIDS - 1, -1, -1):
             last_half(g, slot, 1 - slot)
             slot = 1 - slot
-            exchange(slot)
+            exchange(slot, max(g - 1, 0))
         rz, iz = image(slot, 1 - slot)
         slot = 1 - slot
-        start(slot)
+        start(slot, 0)
         top = jnp.sum(rz, axis=0, keepdims=True)
         bot = jnp.sum(iz, axis=0, keepdims=True)
         own = jnp.where(row == 0, bc_row(top), jnp.where(row == 1, bc_row(bot), 0.0))
@@ -373,7 +381,7 @@
         def _(d):
             sum_copy(it, d).start()
 
-        finish(slot)
+        finish(slot, 0)
 
         @pl.loop(1, devices)
         def _(d):
@@ -399,10 +407,11 @@
 
         @pl.when(it < ITERS - 1)
         def _():
+            for t in range(tiling(0)[1]):
+                w = QC[t] + ratio * WC[t]
+                WC[t] = w
+                XC[t] = XC[t] - alpha * w
             for way in range(2):
-                w = RC[slot, way] + ratio * WC[way]
-                WC[way] = w
-                XC[way] = XC[way] - alpha * w
                 for t in range(SR.shape[2] // rows):
                     at = pl.ds(t * rows, rows)
                     w = RR[slot, way, at, :] + ratio * WR[way, at, :]
@@ -420,6 +429,8 @@
     levels, rows, cols = cotangent.shape
     count, width = fine.shape[0], fine.shape[1]
     devices = sizes[0] * sizes[1] * sizes[2]
+    most = -(-levels // (cols >> GRIDS))
+    fine_tiles = -(-levels // (cols // 2))
     padded = -(-levels // rows) * rows
     if levels > cols or rows != 1 << (GRIDS - 1):
         raise ValueError("unsupported tile")
@@ -440,10 +451,10 @@
             vm(GRIDS, levels + 1), vm(levels), vm(levels),
             vm(GRIDS - 1, levels), vm(GRIDS, levels + 2), vm(levels + 2),
             vm(levels), vm(levels), vm(levels),
-            pltpu.VMEM((2, 2, padded, cols), F32), vm(2, 2),
-            pltpu.VMEM((2, 2, padded, cols), F32), vm(2, 2),
-            pltpu.VMEM((2, padded, cols), F32), vm(2),
-            pltpu.VMEM((2, padded, cols), F32), vm(2),
+            pltpu.VMEM((2, 2, padded, cols), F32), vm(2, most),
+            pltpu.VMEM((2, 2, padded, cols), F32), vm(2, 2, most), vm(most),
+            pltpu.VMEM((2, padded, cols), F32), vm(fine_tiles),
+            pltpu.VMEM((2, padded, cols), F32), vm(fine_tiles),
             vm(), vm(ITERS, devices),
             pltpu.SemaphoreType.DMA((2, 4)), pltpu.SemaphoreType.DMA((2, 4)),
             pltpu.SemaphoreType.DMA((devices - 1,)), pltpu.SemaphoreType.DMA((devices - 1,)),

time: 195 us -> 149 us (0.76)
  Pallas kernels: 187 us -> 141 us
    pallas_call x1, Pallas kernels: 187 us -> 141 us  [per_device(): pl.pallas_call(functools.partial(kernel, sizes, count, width), out_shape=...]
where the time goes in v1:
time: 149 us
  Pallas kernels  141 us (95%)
  local copies, waits for them, and re-layouts  7.16 us (5%)
    pallas_call x1, Pallas kernels, per_device(): pl.pallas_call(functools.partial(kernel, sizes, count, width), out_shape=...  141 us
    unnamed x14, local copies, waits for them, and re-layouts  7.16 us

profile of v1, /device:TPU:0, one launch (start us, length us, event | category | flops | bytes accessed | tf_op | source)
XLA Modules:
  0.0 148.7 jit_solution(1238072791613339975)
XLA Ops:
  0.6 0.0 copy-start
  0.6 0.9 copy-done
  1.6 0.0 copy-start.1
  1.6 1.0 copy-done.1
  2.5 0.0 copy-start.2
  2.6 1.0 copy-done.2
  3.5 0.0 copy-start.3
  3.5 1.0 copy-done.3
  4.5 0.0 copy-start.4
  4.5 1.0 copy-done.4
  5.4 0.0 copy-start.5
  5.4 1.0 copy-done.5
  6.4 140.9 %shard_map.77 = (f32[70,8,128]{2,1,0:T(8,128)S(1)}, f32[70,8,128]{2,1,0:T(8,128)S(1)}) custom-call(f32[70,8,128]{2,1,0:T(8,128)S(1)} %copy-done, f32[70,8,128]{2,1,0:T(8,128)S(1)} %copy-done.1, f32[70,8,128]{2,1,0:T(8,128)S(1)} %copy-done.2, f32[70,8,128]{2,1,0:T(8,128)S(1)} %copy-done.3, f32[69,8,128]{2,1,0:T(8,128)S(1)} %copy-done.5, ...), custom_call_target="tpu_custom_call" | custom-call | tf_op jit(solution)/shard_map/pallas_call | solution.py:443
  147.3 0.7 copy.10
  148.0 0.7 copy.11
Async XLA Ops:
  0.6 1.0 copy-start
  1.6 1.0 copy-start.1
  2.5 1.0 copy-start.2
  3.5 1.0 copy-start.3
  4.5 1.0 copy-start.4
  5.4 1.0 copy-start.5
